TPU v7x, 128 devices: a whole 4x4x4 slice. The times are simulated.
128 devices in a mesh: blk: 16 (over x, y_hi, core), mate: 8 (over z, y_lo).
Axes of the slice: x: 4, y: 4 (y_hi: 2, y_lo: 2; y = y_hi * 2 + y_lo), z: 4, core: 2. Of those that a mesh axis runs over, the one named last changes fastest.
Arguments:
- record: bfloat16 [128, 1024, 2048], P(('blk', 'mate'))
- starts: int32 [128, 2], P(('blk', 'mate')), may hold values from 0 to 1024, as said below
Outputs:
- correlation: float32 [1024, 1024, 512], P('blk', 'mate')
Inputs may be any that keep to these rules, and one draw needn't show every extreme that they name: `starts`: each segment lies inside its window.
All inputs are finite; a program needn't handle non-finite values.
Results may differ from a plain program's by a relative error of at most 0.0059.
Values may be sent and summed in bfloat16 or wider, within the bound.
No kernel may reach another device: no remote copies, remote signals or barrier semaphores. Data moves between devices by JAX's collectives and lax.ppermute only.
A program may use at most 192 MiB of HBM per device.

v0:
```python
import math

import jax
import jax.numpy as jnp
from jax import lax
from jax.sharding import PartitionSpec as P

L = 1024
NB = 128
F0 = 4
LAG = 256


def hann_taper(length):
    times = jnp.arange(length, dtype=jnp.int32).astype(jnp.float32)
    return 0.5 - 0.5 * jnp.cos(2.0 * math.pi / length * (times + 0.5))


def frequency_taper(count):
    ramp = max(count // 8, 1)
    index = jnp.arange(count, dtype=jnp.int32).astype(jnp.float32)
    edge = jnp.minimum(jnp.minimum((index + 0.5) / ramp, (count - index - 0.5) / ramp), 1.0)
    return jnp.sin(0.5 * math.pi * edge) ** 2


def dft_table(length):
    times = jnp.arange(length, dtype=jnp.int32)[:, None]
    bins = F0 + jnp.arange(NB, dtype=jnp.int32)[None, :]
    phase = 2.0 * math.pi / length * (times * bins % length).astype(jnp.float32)
    return jnp.concatenate([jnp.cos(phase), -jnp.sin(phase)], 1).astype(jnp.bfloat16)


def lag_table(length):
    bins = F0 + jnp.arange(NB, dtype=jnp.int32)[:, None]
    shifts = jnp.arange(2 * LAG, dtype=jnp.int32)[None, :] - LAG
    phase = 2.0 * math.pi / length * (bins * shifts % length).astype(jnp.float32)
    return jnp.concatenate([jnp.cos(phase), -jnp.sin(phase)], 0).astype(jnp.bfloat16)


def whiten(segs):
    length = segs.shape[-1]
    lead = segs.shape[:-1]
    flat = segs.reshape(-1, length).astype(jnp.float32)
    centred = flat - jnp.mean(flat, axis=1, keepdims=True)
    scaled = centred * lax.rsqrt(jnp.mean(centred * centred, axis=1, keepdims=True) + 1e-05)
    tapered = (scaled * hann_taper(length)[None, :]).astype(jnp.bfloat16)
    spectrum = jnp.dot(tapered, dft_table(length), preferred_element_type=jnp.float32)
    count = spectrum.shape[1] // 2
    power = spectrum[:, :count] ** 2 + spectrum[:, count:] ** 2
    level = jnp.mean(power, axis=1, keepdims=True)
    gain = frequency_taper(count)[None, :] / jnp.sqrt(power + 0.05 * level + 1e-05)
    whitened = spectrum * jnp.concatenate([gain, gain], 1)
    return whitened.astype(jnp.bfloat16).reshape(lead + (2 * count,))


def pairwise_products(rows, cols, form):
    count = rows.shape[-1] // 2
    real_a, imag_a = (rows[..., :count], rows[..., count:])
    real_b, imag_b = (cols[..., :count], cols[..., count:])
    real = jnp.einsum(form, real_a, real_b, preferred_element_type=jnp.float32)
    real = real + jnp.einsum(form, imag_a, imag_b, preferred_element_type=jnp.float32)
    imag = jnp.einsum(form, imag_a, real_b, preferred_element_type=jnp.float32)
    imag = imag - jnp.einsum(form, real_a, imag_b, preferred_element_type=jnp.float32)
    return jnp.concatenate([real, imag], -1)


def per_device(record, starts):
    window = record[0]
    seg_count = starts.shape[1]
    segs = jax.vmap(lambda begin: lax.dynamic_slice_in_dim(window, begin, L, 1))(starts[0])
    blocks = lax.axis_size("blk")
    groups = lax.axis_size("mate")
    channels = window.shape[0]
    block_width = channels // blocks
    group_width = channels // groups
    row_spec = whiten(lax.all_to_all(segs, "blk", split_axis=1, concat_axis=0, tiled=True))
    row_spec = row_spec.reshape(blocks, seg_count, block_width, row_spec.shape[-1])
    rows_full = lax.all_gather(row_spec[None], "mate", axis=0, tiled=True)
    width = rows_full.shape[-1]
    col_spec = whiten(lax.all_to_all(segs, "mate", split_axis=1, concat_axis=0, tiled=True))
    col_spec = col_spec.reshape(groups, seg_count, group_width, width)
    cross = pairwise_products(
        rows_full, lax.all_gather(col_spec[None], "blk", axis=0, tiled=True), "mbsif,bmsjf->ijf"
    )
    rounded = cross.astype(jnp.bfloat16).reshape(-1, width)
    factor = 1.0 / math.sqrt(blocks * groups * seg_count * (width // 2))
    lagged = jnp.dot(rounded, lag_table(L), preferred_element_type=jnp.float32) * factor
    return lagged.reshape(block_width, group_width, -1)


def solution(mesh):
    placed = (P(("blk", "mate"), None, None), P(("blk", "mate"), None))
    return jax.shard_map(
        per_device, mesh=mesh, in_specs=placed, out_specs=P("blk", "mate", None), check_vma=False
    )
```

profile of v0, /device:TPU:1, one launch (start us, length us, event | category | flops | bytes accessed | tf_op | source)
XLA Modules:
  0.0 552.3 jit_solution(9883679152435040678)
XLA Ops:
  6.5 0.7 compare_select_fusion
  7.4 10.7 %while.1 = (s32[]{:T(128)}, bf16[1024,2048]{1,0:T(8,128)(2,1)}, s32[2,2]{1,0:T(2,128)S(1)}, bf16[2,1024,1024]{2,1,0:T(8,128)(2,1)}, s32[]{:T(128)}) while((s32[]{:T(128)}, bf16[1024,2048]{1,0:T(8,128)(2,1)}, s32[2,2]{1,0:T(2,128)S(1)}, bf16[2,1024,1024]{2,1,0:T(8,128)(2,1)}, s32[]{:T(128)}) %tuple.36), condition=%wide.while_cond, body=%wide.while_body.sunk | while | flops 2 | bytes 4195417 | solution.py:70
  7.4 0.7 slice.84
  8.0 4.7 bitcast_dynamic-update-slice_fusion.2
  12.7 0.7 slice.84
  13.4 4.7 bitcast_dynamic-update-slice_fusion.2
  18.1 6.5 %copy.17 = bf16[2,1024,1024]{2,0,1:T(2,128)(2,1)S(1)} copy(bf16[2,1024,1024]{2,1,0:T(8,128)(2,1)} %get-tuple-element.12) | data formatting | bytes 8388608 | tf_op jit(solution)/shard_map/vmap()/gather | solution.py:70
  24.6 2.0 copy-done
  26.6 55.9 %all_to_all.8 = bf16[2,1024,1024]{2,0,1:T(2,128)(2,1)} all-to-all(bf16[2,1024,1024]{2,0,1:T(2,128)(2,1)S(1)} %copy.17), channel_id=1, replica_groups=mesh['blk'=16,'mate'=8] {'mate'}, dimensions={1} | all-to-all | bytes 8388608 | tf_op jit(solution)/shard_map/all_to_all | solution.py:80
  82.5 8.5 %all-to-all-start.1 = ((bf16[2,1024,1024]{2,0,1:T(2,128)(2,1)}), bf16[2,1024,1024]{2,0,1:T(2,128)(2,1)}, u32[]{:S(2)}, u32[]{:S(2)}) async-start(bf16[2,1024,1024]{2,0,1:T(2,128)(2,1)} %copy-done), calls=%async_computation.1 | async-start | bytes 8388608 | tf_op jit(solution)/shard_map/all_to_all | solution.py:76
  91.1 0.2 all-gather.5.cloned.1.call-start
  91.4 2.2 cosine_convert_fusion
  93.6 4.1 fusion.39
  97.7 0.6 fusion.6
  98.4 1.4 multiply_reduce_fusion.1
  99.8 4.1 copy.19
  103.9 39.9 %all-to-all-done.1 = bf16[2,1024,1024]{2,0,1:T(2,128)(2,1)} async-done(((bf16[2,1024,1024]{2,0,1:T(2,128)(2,1)}), bf16[2,1024,1024]{2,0,1:T(2,128)(2,1)}, u32[]{:S(2)}, u32[]{:S(2)}) %all-to-all-start.1) | async-done | bytes 4194336 | tf_op jit(solution)/shard_map/all_to_all | solution.py:76
  143.8 7.5 %fusion.38 = (bf16[2,1024,1024]{2,1,0:T(8,128)(2,1)S(1)}, f32[16,2,64,1024]{3,2,0,1:T(8,128)}) fusion(bf16[2,1024,1024]{2,0,1:T(2,128)(2,1)} %all-to-all-done.1), kind=kLoop, calls=%fused_computation.83 | loop fusion | flops 2097152 | bytes 16777216 | tf_op jit(solution)/shard_map/all_to_all | solution.py:76
  151.3 0.6 fusion.7
  151.9 1.4 multiply_reduce_fusion
  153.6 4.4 copy.25
  158.0 0.1 slice-done
  158.1 1.3 slice-done.1
  159.4 3.7 fusion.2
  163.1 3.5 fusion.23
  166.6 0.3 fusion.32
  167.0 1.3 fusion.24
  168.3 0.3 fusion.31
  168.7 0.7 rsqrt_multiply_fusion
  169.4 1.9 fusion.13
  171.5 0.7 all-gather.3.cloned.1.call-update
  172.2 1.5 cosine_convert_fusion.1
  173.6 171.0 %all-gather.5.cloned.1.call-done = bf16[8,16,2,64,256]{4,3,2,1,0:T(8,128)(2,1)} async-done(((bf16[1,16,2,64,256]{4,3,2,1,0:T(8,128)(2,1)}), bf16[8,16,2,64,256]{4,3,2,1,0:T(8,128)(2,1)}) %all-gather.5.cloned.1.call-update) | async-done | bytes 8388624 | tf_op jit(solution)/shard_map/all_gather | solution.py:78
  344.7 7.9 %fusion.37 = (bf16[8,16,2,64,128]{4,3,2,1,0:T(8,128)(2,1)}, bf16[8,16,2,64,128]{4,3,2,1,0:T(8,128)(2,1)}) fusion(bf16[8,16,2,64,256]{4,3,2,1,0:T(8,128)(2,1)} %all-gather.5.cloned.1.call-done), kind=kLoop, calls=%fused_computation.82 | loop fusion | bytes 16777216 | tf_op jit(solution)/shard_map/slice | solution.py:58
  352.6 12.9 %copy.36 = bf16[8,16,2,64,128]{3,1,2,4,0:T(8,128)(2,1)} copy(bf16[8,16,2,64,128]{4,3,2,1,0:T(8,128)(2,1)} %get-tuple-element.39) | data formatting | bytes 8388608
  365.5 12.9 %copy.38 = bf16[8,16,2,64,128]{3,1,2,4,0:T(8,128)(2,1)} copy(bf16[8,16,2,64,128]{4,3,2,1,0:T(8,128)(2,1)} %get-tuple-element.40) | data formatting | bytes 8388608
  378.4 80.4 %all-gather.3.cloned.1.call-done = bf16[16,8,2,128,256]{4,3,2,1,0:T(8,128)(2,1)} async-done(((bf16[1,8,2,128,256]{4,3,2,1,0:T(8,128)(2,1)}), bf16[16,8,2,128,256]{4,3,2,1,0:T(8,128)(2,1)}) %all-gather.3.cloned.1.call-update) | async-done | bytes 16777232 | tf_op jit(solution)/shard_map/all_gather | solution.py:83
  458.8 11.9 %fusion.36 = (bf16[16,8,2,128,128]{4,3,2,1,0:T(8,128)(2,1)}, bf16[16,8,2,128,128]{4,3,2,1,0:T(8,128)(2,1)}) fusion(bf16[16,8,2,128,256]{4,3,2,1,0:T(8,128)(2,1)} %all-gather.3.cloned.1.call-done), kind=kLoop, calls=%fused_computation.81 | loop fusion | bytes 33554432 | tf_op jit(solution)/shard_map/slice | solution.py:59
  470.8 12.4 %copy.35 = bf16[16,8,2,128,128]{3,0,2,4,1:T(8,128)(2,1)} copy(bf16[16,8,2,128,128]{4,3,2,1,0:T(8,128)(2,1)} %get-tuple-element.38) | data formatting | bytes 16777216
  483.2 12.7 %copy.37 = bf16[16,8,2,128,128]{3,0,2,4,1:T(8,128)(2,1)} copy(bf16[16,8,2,128,128]{4,3,2,1,0:T(8,128)(2,1)} %get-tuple-element.37) | data formatting | bytes 16777216
  495.9 10.7 %fusion.40 = f32[128,128,64,1,1]{1,2,4,0,3:T(8,128)} fusion(bf16[16,8,2,128,128]{3,0,2,4,1:T(8,128)(2,1)} %copy.35, bf16[8,16,2,64,128]{3,1,2,4,0:T(8,128)(2,1)} %copy.36), kind=kOutput, calls=%fused_computation.85 | convolution fusion | flops 536870912 | bytes 16777216 | tf_op jit(solution)/shard_map/mbsif,bmsjf->ijf/dot_general | solution.py:60
  506.6 10.7 %fusion.41 = f32[128,128,64,1,1]{1,2,4,0,3:T(8,128)} fusion(bf16[16,8,2,128,128]{3,0,2,4,1:T(8,128)(2,1)} %copy.35, bf16[8,16,2,64,128]{3,1,2,4,0:T(8,128)(2,1)} %copy.38), kind=kOutput, calls=%fused_computation.86 | convolution fusion | flops 536870912 | bytes 16777216 | tf_op jit(solution)/shard_map/mbsif,bmsjf->ijf/dot_general | solution.py:62
  517.3 8.8 %fusion.12 = bf16[128,128,64]{1,2,0:T(8,128)(2,1)S(1)} fusion(f32[128,128,64,1,1]{1,2,4,0,3:T(8,128)} %fusion.40, bf16[16,8,2,128,128]{3,0,2,4,1:T(8,128)(2,1)} %copy.37, bf16[8,16,2,64,128]{3,1,2,4,0:T(8,128)(2,1)} %copy.38), kind=kOutput, calls=%fused_computation.23 | convolution fusion | flops 538968064 | bytes 18874368 | tf_op jit(solution)/shard_map/mbsif,bmsjf->ijf/dot_general | solution.py:61
  526.2 1.8 copy.49
  528.0 0.4 copy-done.1
  528.4 7.4 %fusion.11 = bf16[128,128,64]{1,2,0:T(8,128)(2,1)S(1)} fusion(f32[128,128,64,1,1]{1,2,4,0,3:T(8,128)S(1)} %copy-done.1, bf16[16,8,2,128,128]{3,0,2,4,1:T(8,128)(2,1)} %copy.37, bf16[8,16,2,64,128]{3,1,2,4,0:T(8,128)(2,1)} %copy.36), kind=kOutput, calls=%fused_computation.21 | convolution fusion | flops 538968064 | bytes 18874368 | tf_op jit(solution)/shard_map/mbsif,bmsjf->ijf/dot_general | solution.py:63
  535.8 1.8 copy.48
  537.6 7.5 %convolution_multiply_fusion = f32[8192,512]{1,0:T(8,128)} fusion(bf16[8192,128]{0,1:T(8,128)(2,1)S(1)} %bitcast.101, bf16[8192,128]{0,1:T(8,128)(2,1)S(1)} %bitcast.100, bf16[128,512]{1,0:T(8,128)(2,1)S(1)} %get-tuple-element.48, bf16[128,512]{1,0:T(8,128)(2,1)S(1)} %get-tuple-element.47), kind=kOutput, calls=%fused_computation.2 | convolution fusion | flops 2160590848 | bytes 21233664 | tf_op jit(solution)/shard_map/dot_general | solution.py:87
  (28 shorter events, 0.6 us)
Async XLA Ops:
  24.6 2.0 copy-start
  82.5 61.2 %all-to-all-start.1 = ((bf16[2,1024,1024]{2,0,1:T(2,128)(2,1)}), bf16[2,1024,1024]{2,0,1:T(2,128)(2,1)}, u32[]{:S(2)}, u32[]{:S(2)}) async-start(bf16[2,1024,1024]{2,0,1:T(2,128)(2,1)} %copy-done), calls=%async_computation.1 | async-start | bytes 8388608 | tf_op jit(solution)/shard_map/all_to_all | solution.py:76
  91.1 253.6 %all-gather.5.cloned.1.call-start = ((), (), s32[]{:S(2)}) async-start(), calls=%async_computation.3 | async-start | bytes 9437184 | tf_op jit(solution)/shard_map/all_gather | solution.py:78
  153.6 4.6 slice-start
  153.6 5.9 %slice-start.1 = ((s8[8388608]{0:T(1024)(128)(4,1)}), s8[4194304]{0:T(1024)(128)(4,1)S(1)}, s32[]{:S(2)}) async-start(s8[8388608]{0:T(1024)(128)(4,1)} %bitcast.97), calls=%async_computation.5 | async-start | bytes 8388608
  171.4 287.4 %all-gather.3.cloned.1.call-start = ((), (), s32[]{:S(2)}) async-start(), calls=%async_computation.2 | async-start | bytes 17825792 | tf_op jit(solution)/shard_map/all_gather | solution.py:83
  526.2 2.2 copy-start.1
Sparse Core Ops, SparseCore 0:
  171.5 173.1 all-gather.4
  347.1 111.6 all-gather.2
where the time goes:
time: 558 us; the launch traced here: 552 us
  waiting for transfers between devices  292 us (52%)
  local copies, waits for them, and re-layouts  104 us (19%)
  blocking collectives  55.9 us (10%)
  matrix products  50 us (9%)
  other arithmetic  27.2 us (5%)
  between operations  14.1 us (3%)
  starting transfers between devices  8.77 us (2%)
    all_gather x1, waiting for transfers between devices, per_device(): rows_full = lax.all_gather(row_spec[None], 'mate', axis=0, tiled=True)  171 us
    all_gather x1, waiting for transfers between devices, per_device(): lax.all_gather(col_spec[None], 'blk', axis=0, tiled=True)  80.4 us
    unnamed x15, local copies, waits for them, and re-layouts  58.5 us
    all_to_all x1, blocking collectives, per_device(): lax.all_to_all(segs, 'mate', split_axis=1, concat_axis=0, tiled=True)  55.9 us
    all_to_all x1, waiting for transfers between devices, per_device(): lax.all_to_all(segs, 'blk', split_axis=1, concat_axis=0, tiled=True)  39.9 us
    slice x1, local copies, waits for them, and re-layouts, pairwise_products(): real_b, imag_b = (cols[..., :count], cols[..., count:])  11.9 us
  transfers between devices with their start and end apart: 3, of which 3 were waited for; matrix products, arithmetic and copies ran while one was open for 9% of the time, Pallas kernels for 0%

commit v1 on v0

v1 whole, which is shorter than its diff:
```python
import functools
import math

import jax
import jax.numpy as jnp
import ml_dtypes
import numpy as np
from jax import lax
from jax.experimental import pallas as pl
from jax.experimental.pallas import tpu as pltpu
from jax.sharding import PartitionSpec as P

L = 1024
NB = 128
F0 = 4
LAG = 256
CH = 1024
SEGS = 2
PARTS = 2
LANES = 128
BOTH = ("blk", "mate")

NT = (((1,), (1,)), ((), ()))


def hann_taper(length):
    times = np.arange(length, dtype=np.float64)
    return (0.5 - 0.5 * np.cos(2.0 * math.pi / length * (times + 0.5))).astype(np.float32)


def frequency_taper(count):
    ramp = max(count // 8, 1)
    index = np.arange(count, dtype=np.float64)
    edge = np.minimum(np.minimum((index + 0.5) / ramp, (count - index - 0.5) / ramp), 1.0)
    return (np.sin(0.5 * math.pi * edge) ** 2).astype(np.float32)


def dft_table(length):
    times = np.arange(length)[:, None]
    bins = F0 + np.arange(NB)[None, :]
    phase = 2.0 * math.pi / length * (times * bins % length)
    table = np.concatenate([np.cos(phase), -np.sin(phase)], 1)
    return table.astype(np.float32).astype(ml_dtypes.bfloat16)


def lag_table(length):
    bins = F0 + np.arange(NB)[:, None]
    shifts = np.arange(2 * LAG)[None, :] - LAG
    phase = 2.0 * math.pi / length * (bins * shifts % length)
    table = np.stack([np.cos(phase), -np.sin(phase)], 1).reshape(2 * NB, 2 * LAG)
    return table.astype(np.float32).astype(ml_dtypes.bfloat16)


WCH = 256
WROWS = 32
BLOCKS = CH // LANES
ROWS = BLOCKS * SEGS * PARTS


def whiten_kernel(starts, record, dft, hann, band, out, turned, taper, tapered, held):
    step = pl.program_id(0)

    @pl.when(step == 0)
    def _():
        table = dft[...].astype(jnp.float32)
        for s in range(SEGS):
            shift = lax.rem(starts[0, s], L)
            turned[s] = pltpu.roll(table, shift, 1).astype(jnp.bfloat16)
            taper[s] = pltpu.roll(hann[...], shift, 1)

    late = lax.broadcasted_iota(jnp.int32, (WROWS, L), 1)
    half = lax.rem(step, 2)
    for s in range(SEGS):
        begin = starts[0, s]

        def rows(r, _, s=s, begin=begin):
            at = pl.ds(pl.multiple_of(r * WROWS, WROWS), WROWS)
            first = record[0, at, :L].astype(jnp.float32)
            second = record[0, at, L:].astype(jnp.float32)
            seg = jnp.where(late >= begin, first, second)
            centred = seg - jnp.mean(seg, axis=1, keepdims=True)
            scaled = centred * lax.rsqrt(jnp.mean(centred * centred, axis=1, keepdims=True) + 1e-05)
            tapered[at, :] = (scaled * taper[s, 0:1, :]).astype(jnp.bfloat16)
            return 0

        lax.fori_loop(0, WCH // WROWS, rows, 0, unroll=2)
        spectrum = lax.dot_general(turned[s], tapered[...], NT, preferred_element_type=jnp.float32)
        real, imag = spectrum[:NB], spectrum[NB:]
        power = real * real + imag * imag
        level = jnp.mean(power, axis=0, keepdims=True)
        gain = band[:, 0:1] * lax.rsqrt(power + 0.05 * level + 1e-05)
        for p, part in enumerate((real * gain, imag * gain)):
            for c in range(WCH // LANES):
                row = (half * (WCH // LANES) + c) * SEGS * PARTS + s * PARTS + p
                held[pl.ds(row, NB, stride=ROWS // 2), :] = part[:, c * LANES : (c + 1) * LANES]

    @pl.when(half == 1)
    def _():
        out[...] = held[...].reshape(NB, ROWS // 2, LANES).astype(jnp.bfloat16)


def whiten(record, starts):
    return pl.pallas_call(
        whiten_kernel,
        grid=(CH // WCH,),
        in_specs=[
            pl.BlockSpec(memory_space=pltpu.SMEM),
            pl.BlockSpec((1, WCH, 2 * L), lambda i: (0, i, 0)),
            pl.BlockSpec((2 * NB, L), lambda i: (0, 0)),
            pl.BlockSpec((8, L), lambda i: (0, 0)),
            pl.BlockSpec((NB, LANES), lambda i: (0, 0)),
        ],
        out_specs=pl.BlockSpec((NB, ROWS // 2, LANES), lambda i: (0, i // 2, 0)),
        out_shape=jax.ShapeDtypeStruct((NB, ROWS, LANES), jnp.bfloat16),
        scratch_shapes=[
            pltpu.VMEM((SEGS, 2 * NB, L), jnp.bfloat16),
            pltpu.VMEM((SEGS, 8, L), jnp.float32),
            pltpu.VMEM((WCH, L), jnp.bfloat16),
            pltpu.VMEM((NB * ROWS // 2, LANES), jnp.float32),
        ],
        compiler_params=pltpu.CompilerParams(vmem_limit_bytes=48 * 1024 * 1024),
        name="whiten",
    )(
        starts,
        record,
        jnp.asarray(np.ascontiguousarray(dft_table(L).T)),
        jnp.asarray(np.tile(hann_taper(L)[None], (8, 1))),
        jnp.asarray(np.tile(frequency_taper(NB)[:, None], (1, LANES))),
    )


CROWS = 128


def cross_kernel(windows, spectra, out, wide, left, right):
    step = pl.program_id(0)
    depth = SEGS * windows

    @pl.when(step == 0)
    def _():
        wide[...] = spectra[...].reshape(windows * ROWS, LANES).astype(jnp.float32)
        for c in range(BLOCKS):
            chans = pl.ds(c * LANES, LANES)
            other = pl.ds(CH + c * LANES, LANES)
            for s in range(SEGS):
                for p in range(PARTS):
                    row = c * SEGS * PARTS + s * PARTS + p
                    block = wide[pl.ds(row, windows, stride=ROWS), :]
                    at = pl.ds(p * depth + s * windows, windows)
                    mirror = pl.ds((1 - p) * depth + s * windows, windows)
                    right[at, chans] = block.astype(jnp.bfloat16)
                    right[mirror, other] = (block if p == 0 else -block).astype(jnp.bfloat16)
                    left[chans, at] = block.T.astype(jnp.bfloat16)

    rows = left[pl.ds(pl.multiple_of(step * CROWS, CROWS), CROWS), :]
    for p in range(PARTS):
        product = jnp.dot(rows, right[:, p * CH : (p + 1) * CH], preferred_element_type=jnp.float32)
        product = product.astype(jnp.bfloat16)
        width = out.shape[4]
        for b in range(out.shape[0]):
            for m in range(out.shape[1]):
                out[b, m, p] = product[
                    b * out.shape[3] : (b + 1) * out.shape[3], m * width : (m + 1) * width
                ]


def cross(spectra, blocks, groups):
    windows = spectra.shape[0]
    height, width = CH // blocks, CH // groups
    depth = SEGS * windows
    per = CROWS // height
    return pl.pallas_call(
        functools.partial(cross_kernel, windows),
        grid=(CH // CROWS,),
        in_specs=[pl.BlockSpec((windows, ROWS, LANES), lambda i: (0, 0, 0))],
        out_specs=pl.BlockSpec((per, groups, PARTS, height, width), lambda i: (i, 0, 0, 0, 0)),
        out_shape=jax.ShapeDtypeStruct((blocks, groups, PARTS, height, width), jnp.bfloat16),
        scratch_shapes=[
            pltpu.VMEM((windows * ROWS, LANES), jnp.float32),
            pltpu.VMEM((CH, PARTS * depth), jnp.bfloat16),
            pltpu.VMEM((PARTS * depth, PARTS * CH), jnp.bfloat16),
        ],
        compiler_params=pltpu.CompilerParams(vmem_limit_bytes=48 * 1024 * 1024),
        name="cross",
    )(spectra)


LROWS = 16
LSTEP = 4


def lag_kernel(factor, cross_in, table, out, wide):
    inner = pl.program_id(1)

    @pl.when(inner == 0)
    def _():
        wide[...] = cross_in[...].reshape(wide.shape).astype(jnp.float32)

    for r in range(LSTEP):
        block = wide[pl.ds(inner * LSTEP + r, 2 * NB, stride=LROWS), :]
        lagged = jnp.dot(block.T.astype(jnp.bfloat16), table[...], preferred_element_type=jnp.float32)
        out[r] = lagged * factor


def lag(received, factor):
    bins, height, width = received.shape
    return pl.pallas_call(
        functools.partial(lag_kernel, factor),
        grid=(height // LROWS, LROWS // LSTEP),
        in_specs=[
            pl.BlockSpec((bins, LROWS, width), lambda i, j: (0, i, 0)),
            pl.BlockSpec((bins, 2 * LAG), lambda i, j: (0, 0)),
        ],
        out_specs=pl.BlockSpec(
            (LSTEP, width, 2 * LAG), lambda i, j: (i * (LROWS // LSTEP) + j, 0, 0)
        ),
        out_shape=jax.ShapeDtypeStruct((height, width, 2 * LAG), jnp.float32),
        scratch_shapes=[pltpu.VMEM((bins * LROWS, width), jnp.float32)],
        compiler_params=pltpu.CompilerParams(vmem_limit_bytes=48 * 1024 * 1024),
        name="lag",
    )(received, jnp.asarray(lag_table(L)))


def per_device(record, starts):
    blocks = lax.axis_size("blk")
    groups = lax.axis_size("mate")
    factor = 1.0 / math.sqrt(blocks * groups * SEGS * NB)
    spectra = lax.all_to_all(whiten(record, starts), BOTH, split_axis=0, concat_axis=0, tiled=True)
    pairs = cross(spectra, blocks, groups)
    pairs = pairs.reshape((blocks * groups,) + pairs.shape[2:])
    received = lax.all_to_all(pairs, BOTH, split_axis=0, concat_axis=0, tiled=True)
    received = received.reshape((-1,) + received.shape[2:])
    return lag(received, factor)


def solution(mesh):
    placed = (P(BOTH, None, None), P(BOTH, None))
    return jax.shard_map(
        per_device, mesh=mesh, in_specs=placed, out_specs=P("blk", "mate", None), check_vma=False
    )
```

time: 558 us -> 126 us (0.23)
  waiting for transfers between devices: 292 us -> 0 us
  local copies, waits for them, and re-layouts: 104 us -> 5.49 us
  matrix products: 50 us -> 0 us
  blocking collectives: 55.9 us -> 87.9 us
  Pallas kernels: 0 us -> 31.4 us
  other arithmetic: 27.2 us -> 0 us
  between operations: 14.1 us -> 0.03 us
  starting transfers between devices: 8.77 us -> 0 us
    all_gather x2 -> x0, waiting for transfers between devices: 251 us -> none  [the longest x1 171 us: per_device(): rows_full = lax.all_gather(row_spec[None], 'mate', axis=0, tiled=True)]
    unnamed x15 -> x12, local copies, waits for them, and re-layouts: 58.5 us -> 5.49 us
    dot_general x7 -> x0, matrix products: 50 us -> none  [the longest x1 10.7 us: pairwise_products(): real = jnp.einsum(form, real_a, real_b, preferred_element_type=jnp.float32)]
    all_to_all x1 -> x0, waiting for transfers between devices: 39.9 us -> none  [per_device(): lax.all_to_all(segs, 'blk', split_axis=1, concat_axis=0, tiled=True)]
    all_to_all x1 -> x2, blocking collectives: 55.9 us -> 87.9 us  [the longest x1 57.4 us: per_device(): lax.all_to_all(pairs, BOTH, split_axis=0, concat_axis=0, tiled=True)]
    pallas_call x0 -> x3, Pallas kernels: none -> 31.4 us  [the longest x1 13.1 us: lag(): pl.pallas_call(functools.partial(lag_kernel, factor), grid=(height // LRO...]
    slice x2 -> x0, local copies, waits for them, and re-layouts: 19.9 us -> none  [the longest x1 11.9 us: pairwise_products(): real_b, imag_b = (cols[..., :count], cols[..., count:])]
    gather x7 -> x0, local copies, waits for them, and re-layouts: 17.2 us -> none
  transfers between devices with their start and end apart: 3 -> 0, of which waited for: 3 -> 0; matrix products, arithmetic and copies ran while one was open for 9% -> 0% of each run, Pallas kernels for 0% -> 0%
where the time goes in v1:
time: 126 us; the launch traced here: 125 us
  blocking collectives  87.9 us (70%)
  Pallas kernels  31.4 us (25%)
  local copies, waits for them, and re-layouts  5.49 us (4%)
    all_to_all x1, blocking collectives, per_device(): lax.all_to_all(pairs, BOTH, split_axis=0, concat_axis=0, tiled=True)  57.4 us
    all_to_all x1, blocking collectives, per_device(): lax.all_to_all(whiten(record, starts), BOTH, split_axis=0, concat_axis=0,...  30.5 us
    pallas_call x1, Pallas kernels, lag(): pl.pallas_call(functools.partial(lag_kernel, factor), grid=(height // LRO...  13.1 us
    pallas_call x1, Pallas kernels, whiten(): pl.pallas_call(whiten_kernel, grid=(CH // WCH,), in_specs=[pl.BlockSpec(m...  12.9 us
    unnamed x12, local copies, waits for them, and re-layouts  5.49 us
    pallas_call x1, Pallas kernels, cross(): pl.pallas_call(functools.partial(cross_kernel, windows), grid=(CH // CROW...  5.33 us

profile of v1, /device:TPU:1, one launch (start us, length us, event | category | flops | bytes accessed | tf_op | source)
XLA Modules:
  0.0 124.8 jit_solution(17835803043215864836)
XLA Ops:
  0.0 0.0 copy-start
  0.0 2.2 %copy-done = bf16[1,1024,2048]{2,1,0:T(8,128)(2,1)S(1)} copy-done((bf16[1,1024,2048]{2,1,0:T(8,128)(2,1)S(1)}, bf16[1,1024,2048]{2,1,0:T(8,128)(2,1)}, u32[]{:S(2)}) %copy-start) | copy-done | bytes 4194328
  2.2 0.0 copy-start.1
  2.2 1.0 copy-done.1
  3.2 0.0 copy-start.3
  3.2 0.8 copy-done.3
  4.1 0.0 copy-start.4
  4.1 0.8 copy-done.4
  4.8 0.0 copy-start.5
  4.8 0.7 copy-done.5
  5.5 12.9 %whiten.1 = bf16[128,32,128]{2,1,0:T(8,128)(2,1)S(1)} custom-call(s32[1,2]{1,0:T(1,128)S(1)} %copy-done.5, bf16[1,1024,2048]{2,1,0:T(8,128)(2,1)S(1)} %copy-done, bf16[256,1024]{1,0:T(8,128)(2,1)S(1)} %copy-done.1, f32[8,1024]{1,0:T(8,128)S(1)} %copy-done.4, f32[128,128]{1,0:T(8,128)S(1)} %copy-done.3), custom_call_target="tpu_custom_call" | custom-call | tf_op jit(solution)/shard_map/whiten/pallas_call | solution.py:103
  18.4 30.5 %all_to_all.10.spectra = bf16[128,32,128]{2,1,0:T(8,128)(2,1)S(1)} all-to-all(bf16[128,32,128]{2,1,0:T(8,128)(2,1)S(1)} %whiten.1), channel_id=1, replica_groups=mesh['blk'=16,'mate'=8] {'blk','mate'}, dimensions={0} | all-to-all | bytes 2097152 | tf_op jit(solution)/shard_map/all_to_all | solution.py:228
  48.9 5.3 %cross.1 = bf16[16,8,2,64,128]{4,3,2,1,0:T(8,128)(2,1)S(1)} custom-call(bf16[128,32,128]{2,1,0:T(8,128)(2,1)S(1)} %all_to_all.10.spectra), custom_call_target="tpu_custom_call" | custom-call | tf_op jit(solution)/shard_map/cross/pallas_call | solution.py:172
  54.2 0.0 copy-start.2
  54.2 57.4 %all_to_all.11 = bf16[128,2,64,128]{3,2,1,0:T(8,128)(2,1)S(1)} all-to-all(bf16[128,2,64,128]{3,2,1,0:T(8,128)(2,1)S(1)} %bitcast.2), channel_id=1, replica_groups=mesh['blk'=16,'mate'=8] {'blk','mate'}, dimensions={0} | all-to-all | bytes 8388608 | tf_op jit(solution)/shard_map/all_to_all | solution.py:231
  111.7 0.0 copy-done.2
  111.7 13.1 %lag.1 = f32[64,128,512]{2,1,0:T(8,128)} custom-call(bf16[256,64,128]{2,1,0:T(8,128)(2,1)S(1)} %bitcast.3, bf16[256,512]{1,0:T(8,128)(2,1)S(1)} %copy-done.2), custom_call_target="tpu_custom_call" | custom-call | tf_op jit(solution)/shard_map/lag/pallas_call | solution.py:207
Async XLA Ops:
  0.0 2.2 %copy-start = (bf16[1,1024,2048]{2,1,0:T(8,128)(2,1)S(1)}, bf16[1,1024,2048]{2,1,0:T(8,128)(2,1)}, u32[]{:S(2)}) copy-start(bf16[1,1024,2048]{2,1,0:T(8,128)(2,1)} %record.1) | copy-start | bytes 12582916
  2.2 1.0 copy-start.1
  3.2 0.8 copy-start.3
  4.1 0.8 copy-start.4
  4.8 0.7 copy-start.5
  54.2 57.4 %copy-start.2 = (bf16[256,512]{1,0:T(8,128)(2,1)S(1)}, bf16[256,512]{1,0:T(8,128)(2,1)}, u32[]{:S(2)}) copy-start(bf16[256,512]{1,0:T(8,128)(2,1)} %constant.11.clone.table) | copy-start | bytes 786436

commit v2 on v1

v2 whole, which is shorter than its diff:
```python
import functools
import math

import jax
import jax.numpy as jnp
import ml_dtypes
import numpy as np
from jax import lax
from jax.experimental import pallas as pl
from jax.experimental.pallas import tpu as pltpu
from jax.sharding import PartitionSpec as P

L = 1024
NB = 128
F0 = 4
LAG = 256
CH = 1024
SEGS = 2
PARTS = 2
LANES = 128
BOTH = ("blk", "mate")

NT = (((1,), (1,)), ((), ()))


def hann_taper(length):
    times = np.arange(length, dtype=np.float64)
    return (0.5 - 0.5 * np.cos(2.0 * math.pi / length * (times + 0.5))).astype(np.float32)


def frequency_taper(count):
    ramp = max(count // 8, 1)
    index = np.arange(count, dtype=np.float64)
    edge = np.minimum(np.minimum((index + 0.5) / ramp, (count - index - 0.5) / ramp), 1.0)
    return (np.sin(0.5 * math.pi * edge) ** 2).astype(np.float32)


def dft_table(length):
    times = np.arange(length)[:, None]
    bins = F0 + np.arange(NB)[None, :]
    phase = 2.0 * math.pi / length * (times * bins % length)
    table = np.concatenate([np.cos(phase), -np.sin(phase)], 1)
    return table.astype(np.float32).astype(ml_dtypes.bfloat16)


def lag_table(length):
    bins = F0 + np.arange(NB)[:, None]
    shifts = np.arange(2 * LAG)[None, :] - LAG
    phase = 2.0 * math.pi / length * (bins * shifts % length)
    table = np.stack([np.cos(phase), -np.sin(phase)], 1).reshape(2 * NB, 2 * LAG)
    return table.astype(np.float32).astype(ml_dtypes.bfloat16)


WCH = 256
WROWS = 32
BLOCKS = CH // LANES
ROWS = BLOCKS * SEGS * PARTS
ANYWHERE = pl.BlockSpec(memory_space=pltpu.HBM)
RESIDENT = pl.BlockSpec(memory_space=pltpu.VMEM)


def whiten_kernel(
    starts_in, record, dft, hann, band, out, starts, raw, table, window, edge, turned, taper, tapered, held,
    raw_sem, sem,
):
    def fetch(i):
        at = pl.ds(pl.multiple_of(i * WCH, WCH), WCH)
        return pltpu.make_async_copy(record.at[0, at], raw.at[at], raw_sem.at[i])

    small = [
        pltpu.make_async_copy(src, dst, sem.at[i])
        for i, (src, dst) in enumerate(((starts_in, starts), (dft, table), (hann, window), (band, edge)))
    ]
    for copy in small:
        copy.start()
    for i in range(CH // WCH):
        fetch(i).start()
    for copy in small:
        copy.wait()
    for s in range(SEGS):
        shift = lax.rem(starts[0, s], L)
        turned[s] = pltpu.roll(table[...].astype(jnp.float32), shift, 1).astype(jnp.bfloat16)
        taper[s] = pltpu.roll(window[...], shift, 1)
    late = lax.broadcasted_iota(jnp.int32, (WROWS, L), 1)

    def block(i, _):
        fetch(i).wait()
        for s in range(SEGS):
            for r in range(WCH // WROWS):
                at = pl.ds(pl.multiple_of(i * WCH + r * WROWS, WROWS), WROWS)
                first = raw[at, :L].astype(jnp.float32)
                second = raw[at, L:].astype(jnp.float32)
                seg = jnp.where(late >= starts[0, s], first, second)
                centred = seg - jnp.mean(seg, axis=1, keepdims=True)
                scaled = centred * lax.rsqrt(jnp.mean(centred * centred, axis=1, keepdims=True) + 1e-05)
                tapered[s, r * WROWS : (r + 1) * WROWS] = (scaled * taper[s, 0:1, :]).astype(jnp.bfloat16)
        for s in range(SEGS):
            spectrum = lax.dot_general(turned[s], tapered[s], NT, preferred_element_type=jnp.float32)
            real, imag = spectrum[:NB], spectrum[NB:]
            power = real * real + imag * imag
            level = jnp.mean(power, axis=0, keepdims=True)
            gain = edge[:, 0:1] * lax.rsqrt(power + 0.05 * level + 1e-05)
            for p, part in enumerate((real * gain, imag * gain)):
                for c in range(WCH // LANES):
                    row = (i * (WCH // LANES) + c) * SEGS * PARTS + s * PARTS + p
                    held[pl.ds(row, NB, stride=ROWS), :] = part[:, c * LANES : (c + 1) * LANES]
        return 0

    lax.fori_loop(0, CH // WCH, block, 0)
    out[...] = held[...].reshape(NB, ROWS, LANES).astype(jnp.bfloat16)


def whiten(record, starts):
    return pl.pallas_call(
        whiten_kernel,
        in_specs=[ANYWHERE] * 5,
        out_specs=RESIDENT,
        out_shape=jax.ShapeDtypeStruct((NB, ROWS, LANES), jnp.bfloat16),
        scratch_shapes=[
            pltpu.SMEM((1, SEGS), jnp.int32),
            pltpu.VMEM((CH, 2 * L), jnp.bfloat16),
            pltpu.VMEM((2 * NB, L), jnp.bfloat16),
            pltpu.VMEM((8, L), jnp.float32),
            pltpu.VMEM((NB, LANES), jnp.float32),
            pltpu.VMEM((SEGS, 2 * NB, L), jnp.bfloat16),
            pltpu.VMEM((SEGS, 8, L), jnp.float32),
            pltpu.VMEM((SEGS, WCH, L), jnp.bfloat16),
            pltpu.VMEM((NB * ROWS, LANES), jnp.float32),
            pltpu.SemaphoreType.DMA((CH // WCH,)),
            pltpu.SemaphoreType.DMA((4,)),
        ],
        compiler_params=pltpu.CompilerParams(vmem_limit_bytes=48 * 1024 * 1024),
        name="whiten",
    )(
        *(
            pltpu.with_memory_space_constraint(x, pltpu.HBM)
            for x in (
                starts,
                record,
                jnp.asarray(np.ascontiguousarray(dft_table(L).T)),
                jnp.asarray(np.tile(hann_taper(L)[None], (8, 1))),
                jnp.asarray(np.tile(frequency_taper(NB)[:, None], (1, LANES))),
            )
        )
    )


CCOLS = 1024
CPITCH = ROWS + 1


def cross_kernel(windows, spectra, out, wide, left, right):
    depth = SEGS * windows
    blocks, _, _, height, width = out.shape
    for w in range(windows):
        wide[CPITCH * w : CPITCH * w + ROWS] = spectra[w].astype(jnp.float32)
    for c in range(BLOCKS):
        chans = pl.ds(c * LANES, LANES)
        other = pl.ds(CH + c * LANES, LANES)
        for s in range(SEGS):
            for p in range(PARTS):
                row = c * SEGS * PARTS + s * PARTS + p
                block = wide[pl.ds(row, windows, stride=CPITCH), :]
                at = pl.ds(p * depth + s * windows, windows)
                mirror = pl.ds((1 - p) * depth + s * windows, windows)
                right[at, chans] = block.astype(jnp.bfloat16)
                right[mirror, other] = (block if p == 0 else -block).astype(jnp.bfloat16)
                left[chans, at] = block.astype(jnp.bfloat16).T
    for p in range(PARTS):

        def columns(n, _, p=p):
            at = pl.ds(pl.multiple_of(p * CH + n * CCOLS, CCOLS), CCOLS)
            product = jnp.dot(left[...], right[:, at], preferred_element_type=jnp.float32)
            product = product.astype(jnp.bfloat16)
            for b in range(blocks):
                for m in range(CCOLS // width):
                    out[b, n * (CCOLS // width) + m, p] = product[
                        b * height : (b + 1) * height, m * width : (m + 1) * width
                    ]
            return 0

        lax.fori_loop(0, CH // CCOLS, columns, 0)


def cross(spectra, blocks, groups):
    windows = spectra.shape[0]
    height, width = CH // blocks, CH // groups
    depth = SEGS * windows
    return pl.pallas_call(
        functools.partial(cross_kernel, windows),
        in_specs=[RESIDENT],
        out_specs=RESIDENT,
        out_shape=jax.ShapeDtypeStruct((blocks, groups, PARTS, height, width), jnp.bfloat16),
        scratch_shapes=[
            pltpu.VMEM((windows * CPITCH, LANES), jnp.float32),
            pltpu.VMEM((CH, PARTS * depth), jnp.bfloat16),
            pltpu.VMEM((PARTS * depth, PARTS * CH), jnp.bfloat16),
        ],
        compiler_params=pltpu.CompilerParams(vmem_limit_bytes=40 * 1024 * 1024),
        name="cross",
    )(spectra)


LROWS = 16
LPITCH = 17
LSTEP = 4
LSLOTS = 8


def lag_kernel(factor, cross_in, table, out, wide, flat, ready, sem):
    bins, height, width = cross_in.shape
    inner = LROWS // LSTEP
    rounds = height // LROWS

    def put(step):
        slot = lax.rem(step, LSLOTS)
        return pltpu.make_async_copy(ready.at[slot], out.at[pl.ds(step * LSTEP, LSTEP)], sem.at[slot])

    def group(g, _):
        at = pl.ds(pl.multiple_of(g * LROWS, LROWS), LROWS)
        for k in range(bins):
            wide[LPITCH * k : LPITCH * k + LROWS, :] = cross_in[k, at, :].astype(jnp.float32)
        for j in range(inner):
            step = g * inner + j
            for r in range(LSTEP):
                block = wide[pl.ds(j * LSTEP + r, bins, stride=LPITCH), :]
                flat[r * width : (r + 1) * width] = block.astype(jnp.bfloat16).T
            lagged = jnp.dot(flat[...], table[...], preferred_element_type=jnp.float32) * factor

            @pl.when(step >= LSLOTS)
            def _():
                put(step - LSLOTS).wait()

            ready[lax.rem(step, LSLOTS)] = lagged.reshape(LSTEP, width, lagged.shape[-1])
            put(step).start()
        return 0

    lax.fori_loop(0, rounds, group, 0)
    for step in range(max(rounds * inner - LSLOTS, 0), rounds * inner):
        put(step).wait()


def lag(received, factor):
    bins, height, width = received.shape
    return pl.pallas_call(
        functools.partial(lag_kernel, factor),
        in_specs=[RESIDENT, RESIDENT],
        out_specs=ANYWHERE,
        out_shape=jax.ShapeDtypeStruct((height, width, 2 * LAG), jnp.float32),
        scratch_shapes=[
            pltpu.VMEM((bins * LPITCH, width), jnp.float32),
            pltpu.VMEM((LSTEP * width, bins), jnp.bfloat16),
            pltpu.VMEM((LSLOTS, LSTEP, width, 2 * LAG), jnp.float32),
            pltpu.SemaphoreType.DMA((LSLOTS,)),
        ],
        compiler_params=pltpu.CompilerParams(vmem_limit_bytes=40 * 1024 * 1024),
        name="lag",
    )(received, jnp.asarray(lag_table(L)))


def per_device(record, starts):
    blocks = lax.axis_size("blk")
    groups = lax.axis_size("mate")
    factor = 1.0 / math.sqrt(blocks * groups * SEGS * NB)
    spectra = lax.all_to_all(whiten(record, starts), BOTH, split_axis=0, concat_axis=0, tiled=True)
    pairs = cross(spectra, blocks, groups)
    pairs = pairs.reshape((blocks * groups,) + pairs.shape[2:])
    received = lax.all_to_all(pairs, BOTH, split_axis=0, concat_axis=0, tiled=True)
    received = received.reshape((-1,) + received.shape[2:])
    return lag(received, factor)


def solution(mesh):
    placed = (P(BOTH, None, None), P(BOTH, None))
    return jax.shard_map(
        per_device, mesh=mesh, in_specs=placed, out_specs=P("blk", "mate", None), check_vma=False
    )
```

time: 126 us -> 109 us (0.87)
  Pallas kernels: 31.4 us -> 19.3 us
  local copies, waits for them, and re-layouts: 5.49 us -> 0.01 us
    pallas_call x3, Pallas kernels: 31.4 us -> 19.3 us  [the longest x1 8.46 us: whiten(): pl.pallas_call(whiten_kernel, in_specs=[ANYWHERE] * 5, out_specs=RESIDENT...]
    unnamed x12 -> x2, local copies, waits for them, and re-layouts: 5.49 us -> 0.01 us
where the time goes in v2:
time: 109 us; the launch traced here: 107 us
  blocking collectives  87.9 us (81%)
  Pallas kernels  19.3 us (18%)
    all_to_all x1, blocking collectives, per_device(): lax.all_to_all(pairs, BOTH, split_axis=0, concat_axis=0, tiled=True)  57.4 us
    all_to_all x1, blocking collectives, per_device(): lax.all_to_all(whiten(record, starts), BOTH, split_axis=0, concat_axis=0,...  30.5 us
    pallas_call x1, Pallas kernels, whiten(): pl.pallas_call(whiten_kernel, in_specs=[ANYWHERE] * 5, out_specs=RESIDENT...  8.46 us
    pallas_call x1, Pallas kernels, lag(): pl.pallas_call(functools.partial(lag_kernel, factor), in_specs=[RESIDENT,...  8.1 us
    pallas_call x1, Pallas kernels, cross(): pl.pallas_call(functools.partial(cross_kernel, windows), in_specs=[RESIDE...  2.76 us

profile of v2, /device:TPU:1, one launch (start us, length us, event | category | flops | bytes accessed | tf_op | source)
XLA Modules:
  0.0 107.2 jit_solution(1873282239434264953)
XLA Ops:
  0.0 8.5 %whiten.1 = bf16[128,32,128]{2,1,0:T(8,128)(2,1)S(1)} custom-call(s32[1,2]{1,0:T(1,128)} %starts_in.1, bf16[1,1024,2048]{2,1,0:T(8,128)(2,1)} %record.1, bf16[256,1024]{1,0:T(8,128)(2,1)} %constant.8.clone.dft, f32[8,1024]{1,0:T(8,128)} %constant.9.clone.hann, f32[128,128]{1,0:T(8,128)} %constant.10.clone.band), custom_call_target="tpu_custom_call" | custom-call | tf_op jit(solution)/shard_map/whiten/pallas_call | solution.py:114
  8.5 30.5 %all_to_all.10.spectra = bf16[128,32,128]{2,1,0:T(8,128)(2,1)S(1)} all-to-all(bf16[128,32,128]{2,1,0:T(8,128)(2,1)S(1)} %whiten.1), channel_id=1, replica_groups=mesh['blk'=16,'mate'=8] {'blk','mate'}, dimensions={0} | all-to-all | bytes 2097152 | tf_op jit(solution)/shard_map/all_to_all | solution.py:265
  38.9 2.8 %cross.1 = bf16[16,8,2,64,128]{4,3,2,1,0:T(8,128)(2,1)S(1)} custom-call(bf16[128,32,128]{2,1,0:T(8,128)(2,1)S(1)} %all_to_all.10.spectra), custom_call_target="tpu_custom_call" | custom-call | tf_op jit(solution)/shard_map/cross/pallas_call | solution.py:189
  41.7 0.0 copy-start
  41.7 57.4 %all_to_all.11 = bf16[128,2,64,128]{3,2,1,0:T(8,128)(2,1)S(1)} all-to-all(bf16[128,2,64,128]{3,2,1,0:T(8,128)(2,1)S(1)} %bitcast.2), channel_id=1, replica_groups=mesh['blk'=16,'mate'=8] {'blk','mate'}, dimensions={0} | all-to-all | bytes 8388608 | tf_op jit(solution)/shard_map/all_to_all | solution.py:268
  99.1 0.0 copy-done
  99.1 8.1 %lag.1 = f32[64,128,512]{2,1,0:T(8,128)} custom-call(bf16[256,64,128]{2,1,0:T(8,128)(2,1)S(1)} %bitcast.3, bf16[256,512]{1,0:T(8,128)(2,1)S(1)} %copy-done), custom_call_target="tpu_custom_call" | custom-call | tf_op jit(solution)/shard_map/lag/pallas_call | solution.py:245
Async XLA Ops:
  41.7 57.4 %copy-start = (bf16[256,512]{1,0:T(8,128)(2,1)S(1)}, bf16[256,512]{1,0:T(8,128)(2,1)}, u32[]{:S(2)}) copy-start(bf16[256,512]{1,0:T(8,128)(2,1)} %constant.11.clone.table) | copy-start | bytes 786436

commit v3 on v2

--- a/solution.py
+++ b/solution.py
@@ -18,7 +18,10 @@
 SEGS = 2
 PARTS = 2
 LANES = 128
-BOTH = ("blk", "mate")
+SPLIT = {"x": 4, "yh": 2, "core": 2, "z": 4, "yl": 2}
+BLK, MATE = ("x", "yh", "core"), ("z", "yl")
+BOTH = BLK + MATE
+TURN = ("x", "core", "z", "yl", "yh")
 
 NT = (((1,), (1,)), ((), ()))
 
@@ -55,14 +58,16 @@
 WROWS = 32
 BLOCKS = CH // LANES
 ROWS = BLOCKS * SEGS * PARTS
+HPITCH = ROWS + 1
 ANYWHERE = pl.BlockSpec(memory_space=pltpu.HBM)
 RESIDENT = pl.BlockSpec(memory_space=pltpu.VMEM)
 
 
 def whiten_kernel(
-    starts_in, record, dft, hann, band, out, starts, raw, table, window, edge, turned, taper, tapered, held,
-    raw_sem, sem,
+    starts_in, record, dft, hann, band, out, starts, raw, table, window, edge, turned, taper, chosen, tapered,
+    held, raw_sem, sem,
 ):
+
     def fetch(i):
         at = pl.ds(pl.multiple_of(i * WCH, WCH), WCH)
         return pltpu.make_async_copy(record.at[0, at], raw.at[at], raw_sem.at[i])
@@ -71,43 +76,69 @@
         pltpu.make_async_copy(src, dst, sem.at[i])
         for i, (src, dst) in enumerate(((starts_in, starts), (dft, table), (hann, window), (band, edge)))
     ]
+    fetch(0).start()
     for copy in small:
         copy.start()
-    for i in range(CH // WCH):
-        fetch(i).start()
+    fetch(1).start()
     for copy in small:
         copy.wait()
     for s in range(SEGS):
         shift = lax.rem(starts[0, s], L)
         turned[s] = pltpu.roll(table[...].astype(jnp.float32), shift, 1).astype(jnp.bfloat16)
         taper[s] = pltpu.roll(window[...], shift, 1)
-    late = lax.broadcasted_iota(jnp.int32, (WROWS, L), 1)
+
+    def prepare(i, s):
+        passed = lax.broadcasted_iota(jnp.int32, (WROWS, L), 1) >= starts[0, s]
+        sums, squares = [], []
+        for r in range(WCH // WROWS):
+            at = pl.ds(pl.multiple_of(i * WCH + r * WROWS, WROWS), WROWS)
+            seg = jnp.where(passed, raw[at, :L], raw[at, L:])
+            chosen[s, r * WROWS : (r + 1) * WROWS] = seg
+            sums.append(jnp.sum(seg.astype(jnp.float32), axis=1, keepdims=True))
+        means = [jnp.broadcast_to(x * (1.0 / L), (WROWS, LANES)) for x in sums]
+        for r in range(WCH // WROWS):
+            seg = chosen[s, r * WROWS : (r + 1) * WROWS].astype(jnp.float32)
+            total = None
+            for t in range(L // LANES):
+                centred = seg[:, t * LANES : (t + 1) * LANES] - means[r]
+                total = centred * centred if total is None else total + centred * centred
+            squares.append(jnp.sum(total, axis=1, keepdims=True))
+        scales = [jnp.broadcast_to(lax.rsqrt(x * (1.0 / L) + 1e-05), (WROWS, LANES)) for x in squares]
+        for r in range(WCH // WROWS):
+            seg = chosen[s, r * WROWS : (r + 1) * WROWS].astype(jnp.float32)
+            for t in range(L // LANES):
+                at = slice(t * LANES, (t + 1) * LANES)
+                scaled = (seg[:, at] - means[r]) * scales[r]
+                tapered[s, pl.ds(pl.multiple_of(i * WCH + r * WROWS, WROWS), WROWS), at] = (scaled * taper[s, 0:1, at]).astype(jnp.bfloat16)
+
+    def transform(s):
+        spectrum = lax.dot_general(turned[s], tapered[s], NT, preferred_element_type=jnp.float32)
+        for c in range(BLOCKS):
+            real, imag = (spectrum[p * NB : (p + 1) * NB, c * LANES : (c + 1) * LANES] for p in range(PARTS))
+            power = real * real + imag * imag
+            level = jnp.mean(power, axis=0, keepdims=True)
+            gain = edge[...] * lax.rsqrt(power + 0.05 * level + 1e-05)
+            for p, part in enumerate((real * gain, imag * gain)):
+                held[pl.ds(c * SEGS * PARTS + s * PARTS + p, NB, stride=HPITCH), :] = part
+
+    count = CH // WCH
 
     def block(i, _):
         fetch(i).wait()
+
+        @pl.when(i + 2 < count)
+        def _():
+            fetch(i + 2).start()
+
         for s in range(SEGS):
-            for r in range(WCH // WROWS):
-                at = pl.ds(pl.multiple_of(i * WCH + r * WROWS, WROWS), WROWS)
-                first = raw[at, :L].astype(jnp.float32)
-                second = raw[at, L:].astype(jnp.float32)
-                seg = jnp.where(late >= starts[0, s], first, second)
-                centred = seg - jnp.mean(seg, axis=1, keepdims=True)
-                scaled = centred * lax.rsqrt(jnp.mean(centred * centred, axis=1, keepdims=True) + 1e-05)
-                tapered[s, r * WROWS : (r + 1) * WROWS] = (scaled * taper[s, 0:1, :]).astype(jnp.bfloat16)
-        for s in range(SEGS):
-            spectrum = lax.dot_general(turned[s], tapered[s], NT, preferred_element_type=jnp.float32)
-            real, imag = spectrum[:NB], spectrum[NB:]
-            power = real * real + imag * imag
-            level = jnp.mean(power, axis=0, keepdims=True)
-            gain = edge[:, 0:1] * lax.rsqrt(power + 0.05 * level + 1e-05)
-            for p, part in enumerate((real * gain, imag * gain)):
-                for c in range(WCH // LANES):
-                    row = (i * (WCH // LANES) + c) * SEGS * PARTS + s * PARTS + p
-                    held[pl.ds(row, NB, stride=ROWS), :] = part[:, c * LANES : (c + 1) * LANES]
+            prepare(i, s)
         return 0
 
-    lax.fori_loop(0, CH // WCH, block, 0)
-    out[...] = held[...].reshape(NB, ROWS, LANES).astype(jnp.bfloat16)
+    lax.fori_loop(0, count, block, 0)
+    for s in range(SEGS):
+        transform(s)
+    for k in range(NB):
+        out[k] = held[HPITCH * k : HPITCH * k + ROWS].astype(jnp.bfloat16)
 
 
 def whiten(record, starts):
@@ -125,7 +156,8 @@
             pltpu.VMEM((SEGS, 2 * NB, L), jnp.bfloat16),
             pltpu.VMEM((SEGS, 8, L), jnp.float32),
             pltpu.VMEM((SEGS, WCH, L), jnp.bfloat16),
-            pltpu.VMEM((NB * ROWS, LANES), jnp.float32),
+            pltpu.VMEM((SEGS, CH, L), jnp.bfloat16),
+            pltpu.VMEM((NB * HPITCH, LANES), jnp.float32),
             pltpu.SemaphoreType.DMA((CH // WCH,)),
             pltpu.SemaphoreType.DMA((4,)),
         ],
@@ -145,13 +177,12 @@
     )
 
 
-CCOLS = 1024
 CPITCH = ROWS + 1
 
 
 def cross_kernel(windows, spectra, out, wide, left, right):
     depth = SEGS * windows
-    blocks, _, _, height, width = out.shape
+    height, width = out.shape[-2:]
     for w in range(windows):
         wide[CPITCH * w : CPITCH * w + ROWS] = spectra[w].astype(jnp.float32)
     for c in range(BLOCKS):
@@ -167,19 +198,14 @@
                 right[mirror, other] = (block if p == 0 else -block).astype(jnp.bfloat16)
                 left[chans, at] = block.astype(jnp.bfloat16).T
     for p in range(PARTS):
-
-        def columns(n, _, p=p):
-            at = pl.ds(pl.multiple_of(p * CH + n * CCOLS, CCOLS), CCOLS)
-            product = jnp.dot(left[...], right[:, at], preferred_element_type=jnp.float32)
-            product = product.astype(jnp.bfloat16)
-            for b in range(blocks):
-                for m in range(CCOLS // width):
-                    out[b, n * (CCOLS // width) + m, p] = product[
-                        b * height : (b + 1) * height, m * width : (m + 1) * width
-                    ]
-            return 0
-
-        lax.fori_loop(0, CH // CCOLS, columns, 0)
+        product = jnp.dot(left[...], right[:, p * CH : (p + 1) * CH], preferred_element_type=jnp.float32)
+        product = product.astype(jnp.bfloat16)
+        for b in range(CH // height):
+            for m in range(CH // width):
+                place = dict(zip(SPLIT, np.unravel_index(b * (CH // width) + m, tuple(SPLIT.values()))))
+                out[tuple(int(place[a]) for a in TURN) + (p,)] = product[
+                    b * height : (b + 1) * height, m * width : (m + 1) * width
+                ]
 
 
 def cross(spectra, blocks, groups):
@@ -190,7 +216,9 @@
         functools.partial(cross_kernel, windows),
         in_specs=[RESIDENT],
         out_specs=RESIDENT,
-        out_shape=jax.ShapeDtypeStruct((blocks, groups, PARTS, height, width), jnp.bfloat16),
+        out_shape=jax.ShapeDtypeStruct(
+            tuple(SPLIT[a] for a in TURN) + (PARTS, height, width), jnp.bfloat16
+        ),
         scratch_shapes=[
             pltpu.VMEM((windows * CPITCH, LANES), jnp.float32),
             pltpu.VMEM((CH, PARTS * depth), jnp.bfloat16),
@@ -203,8 +231,8 @@
 
 LROWS = 16
 LPITCH = 17
-LSTEP = 4
-LSLOTS = 8
+LSTEP = 8
+LSLOTS = 4
 
 
 def lag_kernel(factor, cross_in, table, out, wide, flat, ready, sem):
@@ -258,20 +286,23 @@
     )(received, jnp.asarray(lag_table(L)))
 
 
+def exchange(x):
+    return lax.all_to_all(x, TURN, split_axis=0, concat_axis=0, tiled=True)
+
+
 def per_device(record, starts):
-    blocks = lax.axis_size("blk")
-    groups = lax.axis_size("mate")
+    blocks = lax.axis_size(BLK)
+    groups = lax.axis_size(MATE)
     factor = 1.0 / math.sqrt(blocks * groups * SEGS * NB)
-    spectra = lax.all_to_all(whiten(record, starts), BOTH, split_axis=0, concat_axis=0, tiled=True)
+    spectra = exchange(whiten(record, starts))
     pairs = cross(spectra, blocks, groups)
-    pairs = pairs.reshape((blocks * groups,) + pairs.shape[2:])
-    received = lax.all_to_all(pairs, BOTH, split_axis=0, concat_axis=0, tiled=True)
-    received = received.reshape((-1,) + received.shape[2:])
-    return lag(received, factor)
+    received = exchange(pairs.reshape((blocks * groups,) + pairs.shape[-3:]))
+    return lag(received.reshape((-1,) + received.shape[2:]), factor)
 
 
 def solution(mesh):
+    fine = jax.sharding.Mesh(mesh.devices.reshape(tuple(SPLIT.values())), tuple(SPLIT))
     placed = (P(BOTH, None, None), P(BOTH, None))
     return jax.shard_map(
-        per_device, mesh=mesh, in_specs=placed, out_specs=P("blk", "mate", None), check_vma=False
+        per_device, mesh=fine, in_specs=placed, out_specs=P(BLK, MATE, None), check_vma=False
     )

time: 109 us -> 104 us (0.954); the launches traced: 107 us -> 104 us
  Pallas kernels: 19.3 us -> 17 us
  blocking collectives: 87.9 us -> 86.6 us
    pallas_call x1, Pallas kernels: 8.46 us -> 6.79 us  [whiten(): pl.pallas_call(whiten_kernel, in_specs=[ANYWHERE] * 5, out_specs=RESIDENT...]
    all_to_all x2, blocking collectives: 87.9 us -> 86.6 us  [exchange(): return lax.all_to_all(x, TURN, split_axis=0, concat_axis=0, tiled=True)]
where the time goes in v3:
time: 104 us
  blocking collectives  86.6 us (83%)
  Pallas kernels  17 us (16%)
    all_to_all x2, blocking collectives, exchange(): return lax.all_to_all(x, TURN, split_axis=0, concat_axis=0, tiled=True)  86.6 us
    pallas_call x1, Pallas kernels, lag(): pl.pallas_call(functools.partial(lag_kernel, factor), in_specs=[RESIDENT,...  7.46 us
    pallas_call x1, Pallas kernels, whiten(): pl.pallas_call(whiten_kernel, in_specs=[ANYWHERE] * 5, out_specs=RESIDENT...  6.79 us
    pallas_call x1, Pallas kernels, cross(): pl.pallas_call(functools.partial(cross_kernel, windows), in_specs=[RESIDE...  2.76 us

profile of v3, /device:TPU:1, one launch (start us, length us, event | category | flops | bytes accessed | tf_op | source)
XLA Modules:
  0.0 103.6 jit_solution(6745202024696541165)
XLA Ops:
  0.0 6.8 %whiten.1 = bf16[128,32,128]{2,1,0:T(8,128)(2,1)S(1)} custom-call(s32[1,2]{1,0:T(1,128)} %starts_in.1, bf16[1,1024,2048]{2,1,0:T(8,128)(2,1)} %record.1, bf16[256,1024]{1,0:T(8,128)(2,1)} %constant.8.clone.dft, f32[8,1024]{1,0:T(8,128)} %constant.9.clone.hann, f32[128,128]{1,0:T(8,128)} %constant.10.clone.band), custom_call_target="tpu_custom_call" | custom-call | tf_op jit(solution)/shard_map/whiten/pallas_call | solution.py:145
  6.8 30.8 %all_to_all.10.spectra = bf16[128,32,128]{2,1,0:T(8,128)(2,1)S(1)} all-to-all(bf16[128,32,128]{2,1,0:T(8,128)(2,1)S(1)} %whiten.1), channel_id=1, replica_groups=mesh['x'=4,'yh'=2,'core'=2,'z'=4,'yl'=2] {'x','core','z','yl','yh'}, dimensions={0} | all-to-all | bytes 2097152 | tf_op jit(solution)/shard_map/all_to_all | solution.py:290
  37.6 2.8 %cross.1 = bf16[4,2,4,2,2,2,64,128]{7,6,5,4,3,2,1,0:T(8,128)(2,1)S(1)} custom-call(bf16[128,32,128]{2,1,0:T(8,128)(2,1)S(1)} %all_to_all.10.spectra), custom_call_target="tpu_custom_call" | custom-call | tf_op jit(solution)/shard_map/cross/pallas_call | solution.py:215
  40.4 0.0 copy-start
  40.4 55.8 %all_to_all.11 = bf16[128,2,64,128]{3,2,1,0:T(8,128)(2,1)S(1)} all-to-all(bf16[128,2,64,128]{3,2,1,0:T(8,128)(2,1)S(1)} %bitcast.2), channel_id=1, replica_groups=mesh['x'=4,'yh'=2,'core'=2,'z'=4,'yl'=2] {'x','core','z','yl','yh'}, dimensions={0} | all-to-all | bytes 8388608 | tf_op jit(solution)/shard_map/all_to_all | solution.py:290
  96.2 0.0 copy-done
  96.2 7.5 %lag.1 = f32[64,128,512]{2,1,0:T(8,128)} custom-call(bf16[256,64,128]{2,1,0:T(8,128)(2,1)S(1)} %bitcast.3, bf16[256,512]{1,0:T(8,128)(2,1)S(1)} %copy-done), custom_call_target="tpu_custom_call" | custom-call | tf_op jit(solution)/shard_map/lag/pallas_call | solution.py:273
Async XLA Ops:
  40.4 55.8 %copy-start = (bf16[256,512]{1,0:T(8,128)(2,1)S(1)}, bf16[256,512]{1,0:T(8,128)(2,1)}, u32[]{:S(2)}) copy-start(bf16[256,512]{1,0:T(8,128)(2,1)} %constant.11.clone.table) | copy-start | bytes 786436

commit v4 on v3

--- a/solution.py
+++ b/solution.py
@@ -69,7 +69,7 @@
 ):
 
     def fetch(i):
-        at = pl.ds(pl.multiple_of(i * WCH, WCH), WCH)
+        at = pl.ds(i * WCH, WCH)
         return pltpu.make_async_copy(record.at[0, at], raw.at[at], raw_sem.at[i])
 
     small = [
@@ -84,14 +84,13 @@
         copy.wait()
     for s in range(SEGS):
         shift = lax.rem(starts[0, s], L)
-        turned[s] = pltpu.roll(table[...].astype(jnp.float32), shift, 1).astype(jnp.bfloat16)
         taper[s] = pltpu.roll(window[...], shift, 1)
 
     def prepare(i, s):
         passed = lax.broadcasted_iota(jnp.int32, (WROWS, L), 1) >= starts[0, s]
         sums, squares = [], []
         for r in range(WCH // WROWS):
-            at = pl.ds(pl.multiple_of(i * WCH + r * WROWS, WROWS), WROWS)
+            at = pl.ds(i * WCH + r * WROWS, WROWS)
             seg = jnp.where(passed, raw[at, :L], raw[at, L:])
             chosen[s, r * WROWS : (r + 1) * WROWS] = seg
             sums.append(jnp.sum(seg.astype(jnp.float32), axis=1, keepdims=True))
@@ -109,9 +108,11 @@
             for t in range(L // LANES):
                 at = slice(t * LANES, (t + 1) * LANES)
                 scaled = (seg[:, at] - means[r]) * scales[r]
-                tapered[s, pl.ds(pl.multiple_of(i * WCH + r * WROWS, WROWS), WROWS), at] = (scaled * taper[s, 0:1, at]).astype(jnp.bfloat16)
+                tapered[s, pl.ds(i * WCH + r * WROWS, WROWS), at] = (scaled * taper[s, 0:1, at]).astype(jnp.bfloat16)
 
     def transform(s):
+        shift = lax.rem(starts[0, s], L)
+        turned[s] = pltpu.roll(table[...].astype(jnp.float32), shift, 1).astype(jnp.bfloat16)
         spectrum = lax.dot_general(turned[s], tapered[s], NT, preferred_element_type=jnp.float32)
         for c in range(BLOCKS):
             real, imag = (spectrum[p * NB : (p + 1) * NB, c * LANES : (c + 1) * LANES] for p in range(PARTS))
@@ -123,18 +124,12 @@
 
     count = CH // WCH
 
-    def block(i, _):
+    for i in range(count):
         fetch(i).wait()
-
-        @pl.when(i + 2 < count)
-        def _():
+        if i + 2 < count:
             fetch(i + 2).start()
-
         for s in range(SEGS):
             prepare(i, s)
-        return 0
-
-    lax.fori_loop(0, count, block, 0)
     for s in range(SEGS):
         transform(s)
     for k in range(NB):
@@ -231,8 +226,8 @@
 
 LROWS = 16
 LPITCH = 17
-LSTEP = 8
-LSLOTS = 4
+LSTEP = 16
+LSLOTS = 3
 
 
 def lag_kernel(factor, cross_in, table, out, wide, flat, ready, sem):

time: 104 us -> 103 us (level)
  no operation moved by 1% of the time
where the time goes in v4:
time: 103 us
  blocking collectives  86.6 us (84%)
  Pallas kernels  16.2 us (16%)
    all_to_all x2, blocking collectives, exchange(): return lax.all_to_all(x, TURN, split_axis=0, concat_axis=0, tiled=True)  86.6 us
    pallas_call x1, Pallas kernels, lag(): pl.pallas_call(functools.partial(lag_kernel, factor), in_specs=[RESIDENT,...  7.2 us
    pallas_call x1, Pallas kernels, whiten(): pl.pallas_call(whiten_kernel, in_specs=[ANYWHERE] * 5, out_specs=RESIDENT...  6.25 us
    pallas_call x1, Pallas kernels, cross(): pl.pallas_call(functools.partial(cross_kernel, windows), in_specs=[RESIDE...  2.76 us

profile of v4, /device:TPU:1, one launch (start us, length us, event | category | flops | bytes accessed | tf_op | source)
XLA Modules:
  0.0 102.8 jit_solution(4799178793279107291)
XLA Ops:
  0.0 6.2 %whiten.1 = bf16[128,32,128]{2,1,0:T(8,128)(2,1)S(1)} custom-call(s32[1,2]{1,0:T(1,128)} %starts_in.1, bf16[1,1024,2048]{2,1,0:T(8,128)(2,1)} %record.1, bf16[256,1024]{1,0:T(8,128)(2,1)} %constant.8.clone.dft, f32[8,1024]{1,0:T(8,128)} %constant.9.clone.hann, f32[128,128]{1,0:T(8,128)} %constant.10.clone.band), custom_call_target="tpu_custom_call" | custom-call | tf_op jit(solution)/shard_map/whiten/pallas_call | solution.py:140
  6.3 30.8 %all_to_all.10.spectra = bf16[128,32,128]{2,1,0:T(8,128)(2,1)S(1)} all-to-all(bf16[128,32,128]{2,1,0:T(8,128)(2,1)S(1)} %whiten.1), channel_id=1, replica_groups=mesh['x'=4,'yh'=2,'core'=2,'z'=4,'yl'=2] {'x','core','z','yl','yh'}, dimensions={0} | all-to-all | bytes 2097152 | tf_op jit(solution)/shard_map/all_to_all | solution.py:285
  37.0 2.8 %cross.1 = bf16[4,2,4,2,2,2,64,128]{7,6,5,4,3,2,1,0:T(8,128)(2,1)S(1)} custom-call(bf16[128,32,128]{2,1,0:T(8,128)(2,1)S(1)} %all_to_all.10.spectra), custom_call_target="tpu_custom_call" | custom-call | tf_op jit(solution)/shard_map/cross/pallas_call | solution.py:210
  39.8 0.0 copy-start
  39.8 55.8 %all_to_all.11 = bf16[128,2,64,128]{3,2,1,0:T(8,128)(2,1)S(1)} all-to-all(bf16[128,2,64,128]{3,2,1,0:T(8,128)(2,1)S(1)} %bitcast.2), channel_id=1, replica_groups=mesh['x'=4,'yh'=2,'core'=2,'z'=4,'yl'=2] {'x','core','z','yl','yh'}, dimensions={0} | all-to-all | bytes 8388608 | tf_op jit(solution)/shard_map/all_to_all | solution.py:285
  95.6 0.0 copy-done
  95.6 7.2 %lag.1 = f32[64,128,512]{2,1,0:T(8,128)} custom-call(bf16[256,64,128]{2,1,0:T(8,128)(2,1)S(1)} %bitcast.3, bf16[256,512]{1,0:T(8,128)(2,1)S(1)} %copy-done), custom_call_target="tpu_custom_call" | custom-call | tf_op jit(solution)/shard_map/lag/pallas_call | solution.py:268
Async XLA Ops:
  39.8 55.8 %copy-start = (bf16[256,512]{1,0:T(8,128)(2,1)S(1)}, bf16[256,512]{1,0:T(8,128)(2,1)}, u32[]{:S(2)}) copy-start(bf16[256,512]{1,0:T(8,128)(2,1)} %constant.11.clone.table) | copy-start | bytes 786436

commit v5 on v4

--- a/solution.py
+++ b/solution.py
@@ -21,7 +21,7 @@
 SPLIT = {"x": 4, "yh": 2, "core": 2, "z": 4, "yl": 2}
 BLK, MATE = ("x", "yh", "core"), ("z", "yl")
 BOTH = BLK + MATE
-TURN = ("x", "core", "z", "yl", "yh")
+TURN = ("yh", "yl", "core", "z", "x")
 
 NT = (((1,), (1,)), ((), ()))
 

time: 103 us -> 102 us (level)
  no operation moved by 1% of the time
where the time goes in v5:
time: 102 us
  blocking collectives  86 us (84%)
  Pallas kernels  16.2 us (16%)
    all_to_all x2, blocking collectives, exchange(): return lax.all_to_all(x, TURN, split_axis=0, concat_axis=0, tiled=True)  86 us
    pallas_call x1, Pallas kernels, lag(): pl.pallas_call(functools.partial(lag_kernel, factor), in_specs=[RESIDENT,...  7.2 us
    pallas_call x1, Pallas kernels, whiten(): pl.pallas_call(whiten_kernel, in_specs=[ANYWHERE] * 5, out_specs=RESIDENT...  6.25 us
    pallas_call x1, Pallas kernels, cross(): pl.pallas_call(functools.partial(cross_kernel, windows), in_specs=[RESIDE...  2.76 us

profile of v5, /device:TPU:1, one launch (start us, length us, event | category | flops | bytes accessed | tf_op | source)
XLA Modules:
  0.0 102.3 jit_solution(7331069469535179133)
XLA Ops:
  0.0 6.2 %whiten.1 = bf16[128,32,128]{2,1,0:T(8,128)(2,1)S(1)} custom-call(s32[1,2]{1,0:T(1,128)} %starts_in.1, bf16[1,1024,2048]{2,1,0:T(8,128)(2,1)} %record.1, bf16[256,1024]{1,0:T(8,128)(2,1)} %constant.8.clone.dft, f32[8,1024]{1,0:T(8,128)} %constant.9.clone.hann, f32[128,128]{1,0:T(8,128)} %constant.10.clone.band), custom_call_target="tpu_custom_call" | custom-call | tf_op jit(solution)/shard_map/whiten/pallas_call | solution.py:140
  6.3 30.6 %all_to_all.10.spectra = bf16[128,32,128]{2,1,0:T(8,128)(2,1)S(1)} all-to-all(bf16[128,32,128]{2,1,0:T(8,128)(2,1)S(1)} %whiten.1), channel_id=1, replica_groups=mesh['x'=4,'yh'=2,'core'=2,'z'=4,'yl'=2] {'yh','yl','core','z','x'}, dimensions={0} | all-to-all | bytes 2097152 | tf_op jit(solution)/shard_map/all_to_all | solution.py:285
  36.8 2.8 %cross.1 = bf16[2,2,2,4,4,2,64,128]{7,6,5,4,3,2,1,0:T(8,128)(2,1)S(1)} custom-call(bf16[128,32,128]{2,1,0:T(8,128)(2,1)S(1)} %all_to_all.10.spectra), custom_call_target="tpu_custom_call" | custom-call | tf_op jit(solution)/shard_map/cross/pallas_call | solution.py:210
  39.6 0.0 copy-start
  39.6 55.4 %all_to_all.11 = bf16[128,2,64,128]{3,2,1,0:T(8,128)(2,1)S(1)} all-to-all(bf16[128,2,64,128]{3,2,1,0:T(8,128)(2,1)S(1)} %bitcast.2), channel_id=1, replica_groups=mesh['x'=4,'yh'=2,'core'=2,'z'=4,'yl'=2] {'yh','yl','core','z','x'}, dimensions={0} | all-to-all | bytes 8388608 | tf_op jit(solution)/shard_map/all_to_all | solution.py:285
  95.1 0.0 copy-done
  95.1 7.2 %lag.1 = f32[64,128,512]{2,1,0:T(8,128)} custom-call(bf16[256,64,128]{2,1,0:T(8,128)(2,1)S(1)} %bitcast.3, bf16[256,512]{1,0:T(8,128)(2,1)S(1)} %copy-done), custom_call_target="tpu_custom_call" | custom-call | tf_op jit(solution)/shard_map/lag/pallas_call | solution.py:268
Async XLA Ops:
  39.6 55.5 %copy-start = (bf16[256,512]{1,0:T(8,128)(2,1)S(1)}, bf16[256,512]{1,0:T(8,128)(2,1)}, u32[]{:S(2)}) copy-start(bf16[256,512]{1,0:T(8,128)(2,1)} %constant.11.clone.table) | copy-start | bytes 786436

commit v6 on v5

--- a/solution.py
+++ b/solution.py
@@ -18,6 +18,7 @@
 SEGS = 2
 PARTS = 2
 LANES = 128
+SPARE = 64
 SPLIT = {"x": 4, "yh": 2, "core": 2, "z": 4, "yl": 2}
 BLK, MATE = ("x", "yh", "core"), ("z", "yl")
 BOTH = BLK + MATE
@@ -152,7 +153,7 @@
             pltpu.VMEM((SEGS, 8, L), jnp.float32),
             pltpu.VMEM((SEGS, WCH, L), jnp.bfloat16),
             pltpu.VMEM((SEGS, CH, L), jnp.bfloat16),
-            pltpu.VMEM((NB * HPITCH, LANES), jnp.float32),
+            pltpu.VMEM((NB * HPITCH + SPARE, LANES), jnp.float32),
             pltpu.SemaphoreType.DMA((CH // WCH,)),
             pltpu.SemaphoreType.DMA((4,)),
         ],
@@ -215,7 +216,7 @@
             tuple(SPLIT[a] for a in TURN) + (PARTS, height, width), jnp.bfloat16
         ),
         scratch_shapes=[
-            pltpu.VMEM((windows * CPITCH, LANES), jnp.float32),
+            pltpu.VMEM((windows * CPITCH + SPARE, LANES), jnp.float32),
             pltpu.VMEM((CH, PARTS * depth), jnp.bfloat16),
             pltpu.VMEM((PARTS * depth, PARTS * CH), jnp.bfloat16),
         ],
@@ -271,7 +272,7 @@
         out_specs=ANYWHERE,
         out_shape=jax.ShapeDtypeStruct((height, width, 2 * LAG), jnp.float32),
         scratch_shapes=[
-            pltpu.VMEM((bins * LPITCH, width), jnp.float32),
+            pltpu.VMEM((bins * LPITCH + SPARE, width), jnp.float32),
             pltpu.VMEM((LSTEP * width, bins), jnp.bfloat16),
             pltpu.VMEM((LSLOTS, LSTEP, width, 2 * LAG), jnp.float32),
             pltpu.SemaphoreType.DMA((LSLOTS,)),

time: 102 us -> 102 us (level)
  no operation moved by 1% of the time
where the time goes in v6:
time: 102 us
  blocking collectives  86 us (84%)
  Pallas kernels  16.2 us (16%)
    all_to_all x2, blocking collectives, exchange(): return lax.all_to_all(x, TURN, split_axis=0, concat_axis=0, tiled=True)  86 us
    pallas_call x1, Pallas kernels, lag(): pl.pallas_call(functools.partial(lag_kernel, factor), in_specs=[RESIDENT,...  7.2 us
    pallas_call x1, Pallas kernels, whiten(): pl.pallas_call(whiten_kernel, in_specs=[ANYWHERE] * 5, out_specs=RESIDENT...  6.25 us
    pallas_call x1, Pallas kernels, cross(): pl.pallas_call(functools.partial(cross_kernel, windows), in_specs=[RESIDE...  2.76 us

profile of v6, /device:TPU:1, one launch (start us, length us, event | category | flops | bytes accessed | tf_op | source)
XLA Modules:
  0.0 102.3 jit_solution(13301487939794519785)
XLA Ops:
  0.0 6.2 %whiten.1 = bf16[128,32,128]{2,1,0:T(8,128)(2,1)S(1)} custom-call(s32[1,2]{1,0:T(1,128)} %starts_in.1, bf16[1,1024,2048]{2,1,0:T(8,128)(2,1)} %record.1, bf16[256,1024]{1,0:T(8,128)(2,1)} %constant.8.clone.dft, f32[8,1024]{1,0:T(8,128)} %constant.9.clone.hann, f32[128,128]{1,0:T(8,128)} %constant.10.clone.band), custom_call_target="tpu_custom_call" | custom-call | tf_op jit(solution)/shard_map/whiten/pallas_call | solution.py:141
  6.3 30.6 %all_to_all.10.spectra = bf16[128,32,128]{2,1,0:T(8,128)(2,1)S(1)} all-to-all(bf16[128,32,128]{2,1,0:T(8,128)(2,1)S(1)} %whiten.1), channel_id=1, replica_groups=mesh['x'=4,'yh'=2,'core'=2,'z'=4,'yl'=2] {'yh','yl','core','z','x'}, dimensions={0} | all-to-all | bytes 2097152 | tf_op jit(solution)/shard_map/all_to_all | solution.py:286
  36.8 2.8 %cross.1 = bf16[2,2,2,4,4,2,64,128]{7,6,5,4,3,2,1,0:T(8,128)(2,1)S(1)} custom-call(bf16[128,32,128]{2,1,0:T(8,128)(2,1)S(1)} %all_to_all.10.spectra), custom_call_target="tpu_custom_call" | custom-call | tf_op jit(solution)/shard_map/cross/pallas_call | solution.py:211
  39.6 0.0 copy-start
  39.6 55.4 %all_to_all.11 = bf16[128,2,64,128]{3,2,1,0:T(8,128)(2,1)S(1)} all-to-all(bf16[128,2,64,128]{3,2,1,0:T(8,128)(2,1)S(1)} %bitcast.2), channel_id=1, replica_groups=mesh['x'=4,'yh'=2,'core'=2,'z'=4,'yl'=2] {'yh','yl','core','z','x'}, dimensions={0} | all-to-all | bytes 8388608 | tf_op jit(solution)/shard_map/all_to_all | solution.py:286
  95.1 0.0 copy-done
  95.1 7.2 %lag.1 = f32[64,128,512]{2,1,0:T(8,128)} custom-call(bf16[256,64,128]{2,1,0:T(8,128)(2,1)S(1)} %bitcast.3, bf16[256,512]{1,0:T(8,128)(2,1)S(1)} %copy-done), custom_call_target="tpu_custom_call" | custom-call | tf_op jit(solution)/shard_map/lag/pallas_call | solution.py:269
Async XLA Ops:
  39.6 55.5 %copy-start = (bf16[256,512]{1,0:T(8,128)(2,1)S(1)}, bf16[256,512]{1,0:T(8,128)(2,1)}, u32[]{:S(2)}) copy-start(bf16[256,512]{1,0:T(8,128)(2,1)} %constant.11.clone.table) | copy-start | bytes 786436

commit v7 on v6

--- a/solution.py
+++ b/solution.py
@@ -23,6 +23,7 @@
 BLK, MATE = ("x", "yh", "core"), ("z", "yl")
 BOTH = BLK + MATE
 TURN = ("yh", "yl", "core", "z", "x")
+FIRST = ("yl", "z", "core", "yh", "x")
 
 NT = (((1,), (1,)), ((), ()))
 
@@ -134,7 +135,9 @@
     for s in range(SEGS):
         transform(s)
     for k in range(NB):
-        out[k] = held[HPITCH * k : HPITCH * k + ROWS].astype(jnp.bfloat16)
+        place = dict(zip(FIRST, np.unravel_index(k, tuple(SPLIT[a] for a in FIRST))))
+        row = HPITCH * int(np.ravel_multi_index([place[a] for a in TURN], [SPLIT[a] for a in TURN]))
+        out[k] = held[row : row + ROWS].astype(jnp.bfloat16)
 
 
 def whiten(record, starts):
@@ -282,17 +285,17 @@
     )(received, jnp.asarray(lag_table(L)))
 
 
-def exchange(x):
-    return lax.all_to_all(x, TURN, split_axis=0, concat_axis=0, tiled=True)
+def exchange(x, order):
+    return lax.all_to_all(x, order, split_axis=0, concat_axis=0, tiled=True)
 
 
 def per_device(record, starts):
     blocks = lax.axis_size(BLK)
     groups = lax.axis_size(MATE)
     factor = 1.0 / math.sqrt(blocks * groups * SEGS * NB)
-    spectra = exchange(whiten(record, starts))
+    spectra = exchange(whiten(record, starts), FIRST)
     pairs = cross(spectra, blocks, groups)
-    received = exchange(pairs.reshape((blocks * groups,) + pairs.shape[-3:]))
+    received = exchange(pairs.reshape((blocks * groups,) + pairs.shape[-3:]), TURN)
     return lag(received.reshape((-1,) + received.shape[2:]), factor)
 
 

time: 102 us -> 103 us (level)
  no operation moved by 1% of the time
where the time goes in v7:
time: 103 us
  blocking collectives  86.5 us (84%)
  Pallas kernels  16.2 us (16%)
    all_to_all x2, blocking collectives, exchange(): return lax.all_to_all(x, order, split_axis=0, concat_axis=0, tiled=True)  86.5 us
    pallas_call x1, Pallas kernels, lag(): pl.pallas_call(functools.partial(lag_kernel, factor), in_specs=[RESIDENT,...  7.2 us
    pallas_call x1, Pallas kernels, whiten(): pl.pallas_call(whiten_kernel, in_specs=[ANYWHERE] * 5, out_specs=RESIDENT...  6.24 us
    pallas_call x1, Pallas kernels, cross(): pl.pallas_call(functools.partial(cross_kernel, windows), in_specs=[RESIDE...  2.76 us

profile of v7, /device:TPU:1, one launch (start us, length us, event | category | flops | bytes accessed | tf_op | source)
XLA Modules:
  0.0 102.7 jit_solution(16309724829198072916)
XLA Ops:
  0.0 6.2 %whiten.1 = bf16[128,32,128]{2,1,0:T(8,128)(2,1)S(1)} custom-call(s32[1,2]{1,0:T(1,128)} %starts_in.1, bf16[1,1024,2048]{2,1,0:T(8,128)(2,1)} %record.1, bf16[256,1024]{1,0:T(8,128)(2,1)} %constant.8.clone.dft, f32[8,1024]{1,0:T(8,128)} %constant.9.clone.hann, f32[128,128]{1,0:T(8,128)} %constant.10.clone.band), custom_call_target="tpu_custom_call" | custom-call | tf_op jit(solution)/shard_map/whiten/pallas_call | solution.py:144
  6.3 28.9 %all_to_all.10.spectra = bf16[128,32,128]{2,1,0:T(8,128)(2,1)S(1)} all-to-all(bf16[128,32,128]{2,1,0:T(8,128)(2,1)S(1)} %whiten.1), channel_id=1, replica_groups=mesh['x'=4,'yh'=2,'core'=2,'z'=4,'yl'=2] {'yl','z','core','yh','x'}, dimensions={0} | all-to-all | bytes 2097152 | tf_op jit(solution)/shard_map/all_to_all | solution.py:289
  35.1 2.8 %cross.1 = bf16[2,2,2,4,4,2,64,128]{7,6,5,4,3,2,1,0:T(8,128)(2,1)S(1)} custom-call(bf16[128,32,128]{2,1,0:T(8,128)(2,1)S(1)} %all_to_all.10.spectra), custom_call_target="tpu_custom_call" | custom-call | tf_op jit(solution)/shard_map/cross/pallas_call | solution.py:214
  37.9 0.0 copy-start
  37.9 57.6 %all_to_all.11 = bf16[128,2,64,128]{3,2,1,0:T(8,128)(2,1)S(1)} all-to-all(bf16[128,2,64,128]{3,2,1,0:T(8,128)(2,1)S(1)} %bitcast.2), channel_id=1, replica_groups=mesh['x'=4,'yh'=2,'core'=2,'z'=4,'yl'=2] {'yh','yl','core','z','x'}, dimensions={0} | all-to-all | bytes 8388608 | tf_op jit(solution)/shard_map/all_to_all | solution.py:289
  95.5 0.0 copy-done
  95.5 7.2 %lag.1 = f32[64,128,512]{2,1,0:T(8,128)} custom-call(bf16[256,64,128]{2,1,0:T(8,128)(2,1)S(1)} %bitcast.3, bf16[256,512]{1,0:T(8,128)(2,1)S(1)} %copy-done), custom_call_target="tpu_custom_call" | custom-call | tf_op jit(solution)/shard_map/lag/pallas_call | solution.py:272
Async XLA Ops:
  37.9 57.6 %copy-start = (bf16[256,512]{1,0:T(8,128)(2,1)S(1)}, bf16[256,512]{1,0:T(8,128)(2,1)}, u32[]{:S(2)}) copy-start(bf16[256,512]{1,0:T(8,128)(2,1)} %constant.11.clone.table) | copy-start | bytes 786436
